TPU v7x, 256 devices: a whole 4x4x8 slice. The times are simulated.
256 devices in a mesh: users: 32 (over y, z), dims: 8 (over x, core).
Axes of the slice: x: 4, y: 4, z: 8, core: 2. Of those that a mesh axis runs over, the one named last changes fastest.
Arguments:
- user_factors: bfloat16 [65536, 1024], P('users', 'dims'), may hold values from -1.08 to 1.08
- item_factors: bfloat16 [4096, 1024], P('users', 'dims'), may hold values from -1.08 to 1.08
- ratings: bfloat16 [960, 256, 256], P('users'), may hold values from -6 to 6
- tile_coords: int32 [960, 2], P('users'), may hold values from 0 to 15, as said below
- tile_count: int32 [32], P('users'), may hold values from 1 to 30, as said below
- item_gram: bfloat16 [1024, 1024], P(None, 'dims'), as said below
- user_gram: bfloat16 [1024, 1024], P(None, 'dims'), as said below
- user_inverse: float32 [1024, 128], P('dims')
- item_inverse: float32 [1024, 128], P('dims')
Outputs:
- user_new: bfloat16 [65536, 1024], P('users', 'dims')
- item_new: bfloat16 [4096, 1024], P('users', 'dims')
Inputs may be any that keep to these rules, and one draw needn't show every extreme that they name: `tile_coords`: within one slab's 30 slots no pair (tile row, item panel) repeats; column 0 is below 8, column 1 below 16. `tile_count`: some slab has exactly 30 tiles. `item_gram`: Symmetric. `user_gram`: Symmetric.
All inputs are finite; a program needn't handle non-finite values.
Results may differ from a plain program's by a relative error of at most 0.014.
Values may be sent and summed in bfloat16 or wider, within the bound.
A program may use at most 64 MiB of HBM per device.

v0:
```python
import jax
import jax.numpy as jnp
from jax import lax
from jax.sharding import PartitionSpec as P

UNOBSERVED = 256.0
REGULAR = 2.0
HIGHEST = lax.Precision.HIGHEST


def predict(user_tiles, item_tiles):
    partial_value = jnp.einsum(
        "sik,sjk->sij", user_tiles, item_tiles, preferred_element_type=jnp.float32
    )
    return lax.psum(partial_value.astype(jnp.bfloat16), "dims").astype(jnp.float32)


def couple(factors, gram_columns):
    return (
        lax.psum_scatter(
            lax.dot_general(
                gram_columns, factors, (((1,), (1,)), ((), ())), preferred_element_type=jnp.float32
            ).astype(jnp.bfloat16),
            "dims",
            scatter_dimension=0,
            tiled=True,
        )
        .astype(jnp.float32)
        .T
    )


def newton(factors, gradient, inverse):
    update = jnp.dot(gradient, inverse, precision=HIGHEST, preferred_element_type=jnp.float32)
    return (factors.astype(jnp.float32) + update).astype(jnp.bfloat16)


def local(
    user_factors,
    item_factors,
    ratings,
    tile_coords,
    tile_count,
    item_gram,
    user_gram,
    user_inverse,
    item_inverse,
):
    user_rows, block_width = user_factors.shape
    slot_count, tile_size = (ratings.shape[0], ratings.shape[1])
    row_tiles = user_rows // tile_size
    item_block = lax.all_gather(item_factors, "users", axis=0, tiled=True)
    panel_count = item_block.shape[0] // tile_size
    row_index = tile_coords[:, 0]
    panel_index = tile_coords[:, 1]
    live_mask = (lax.iota(jnp.int32, slot_count) < tile_count[0]).astype(jnp.float32)[:, None, None]
    row_hot = (row_index[:, None] == lax.iota(jnp.int32, row_tiles)[None, :]).astype(jnp.float32)
    panel_hot = (panel_index[:, None] == lax.iota(jnp.int32, panel_count)[None, :]).astype(
        jnp.float32
    )
    item_tiles = item_block.reshape(panel_count, tile_size, block_width)[panel_index]
    user_tiles = user_factors.reshape(row_tiles, tile_size, block_width)[row_index]
    rating_values = ratings.astype(jnp.float32)
    errors = (live_mask * (rating_values - predict(user_tiles, item_tiles))).astype(jnp.bfloat16)
    additions = jnp.einsum("sij,sjb->sib", errors, item_tiles, preferred_element_type=jnp.float32)
    observed = jnp.einsum("sr,sib->rib", row_hot, additions, precision=HIGHEST).reshape(
        user_rows, block_width
    )
    gradient = (
        observed
        - UNOBSERVED * couple(user_factors, item_gram)
        - REGULAR * user_factors.astype(jnp.float32)
    )
    user_new = newton(user_factors, gradient, user_inverse)
    new_tiles = user_new.reshape(row_tiles, tile_size, block_width)[row_index]
    errors_new = (live_mask * (rating_values - predict(new_tiles, item_tiles))).astype(jnp.bfloat16)
    item_terms = jnp.einsum(
        "sij,sib->sjb", errors_new, new_tiles, preferred_element_type=jnp.float32
    )
    item_sums = jnp.einsum("sp,sjb->pjb", panel_hot, item_terms, precision=HIGHEST).reshape(
        panel_count * tile_size, block_width
    )
    item_observed = lax.psum_scatter(
        item_sums.astype(jnp.bfloat16), "users", scatter_dimension=0, tiled=True
    ).astype(jnp.float32)
    item_gradient = (
        item_observed
        - UNOBSERVED * couple(item_factors, user_gram)
        - REGULAR * item_factors.astype(jnp.float32)
    )
    item_new = newton(item_factors, item_gradient, item_inverse)
    return (user_new, item_new)


def solution(mesh):
    placed = (
        P("users", "dims"),
        P("users", "dims"),
        P("users", None, None),
        P("users", None),
        P("users"),
        P(None, "dims"),
        P(None, "dims"),
        P("dims", None),
        P("dims", None),
    )
    return jax.shard_map(
        local,
        mesh=mesh,
        in_specs=placed,
        out_specs=(P("users", "dims"), P("users", "dims")),
        check_vma=False,
    )
```

profile of v0, /device:TPU:2, one launch (start us, length us, event | category | flops | bytes accessed | tf_op | source)
XLA Modules:
  0.0 563.1 jit_solution(12424796007652242567)
XLA Ops:
  7.2 0.0 copy-start
  7.2 0.0 all-gather.2.cloned.1.call-start
  7.2 0.7 all-gather.2.cloned.1.call-update
  7.9 0.0 all-reduce.3.cloned.1.call-start
  8.0 0.8 slice_bitcast_fusion
  8.7 3.2 gather_fusion
  11.9 77.9 %all-gather.2.cloned.1.call-done = bf16[4096,128]{1,0:T(8,128)(2,1)} async-done(((bf16[128,128]{1,0:T(8,128)(2,1)}), bf16[4096,128]{1,0:T(8,128)(2,1)}) %all-gather.2.cloned.1.call-update) | async-done | bytes 1048592 | tf_op jit(solution)/shard_map/all_gather | solution.py:52
  89.8 2.1 gather_fusion.1
  91.9 4.6 convolution_convert_fusion.2
  96.5 0.0 copy-start.2
  96.5 0.0 all-reduce.3.cloned.1.call-update
  96.6 0.0 reduce-scatter.10.cloned.1.call-start
  96.6 0.0 copy-done
  96.6 1.0 copy-done.2
  97.6 3.2 convolution_convert_fusion
  100.8 0.0 reduce-scatter.10.cloned.1.call-update
  100.8 0.0 all-reduce.5.cloned.1.call-start
  101.5 67.0 %all-reduce.3.cloned.1.call-done = bf16[30,256,256]{2,1,0:T(8,128)(2,1)} async-done(((bf16[30,256,256]{2,1,0:T(8,128)(2,1)}), bf16[30,256,256]{2,1,0:T(8,128)(2,1)}) %all-reduce.3.cloned.1.call-update) | async-done | bytes 3932176 | tf_op jit(solution)/shard_map/psum | solution.py:15
  168.5 4.7 fusion.10
  173.3 0.0 copy-start.7
  173.3 3.7 fusion.6
  177.0 1.2 copy.14
  178.2 32.5 %reduce-scatter.10.cloned.1.call-done = bf16[128,2048]{1,0:T(8,128)(2,1)} async-done(((bf16[1024,2048]{1,0:T(8,128)(2,1)}), bf16[128,2048]{1,0:T(8,128)(2,1)}) %reduce-scatter.10.cloned.1.call-update) | async-done | bytes 524304
  210.7 2.0 copy.22
  212.7 0.0 copy-done.7
  212.7 2.4 fusion.14
  215.2 0.0 copy-start.3
  215.2 2.2 gather_fusion.2
  217.4 4.6 convolution_convert_fusion.1
  222.0 0.0 copy-done.3
  222.0 0.0 copy-start.4
  222.0 0.0 copy-start.5
  222.0 0.0 copy-start.1
  222.0 0.0 all-reduce.5.cloned.1.call-update
  222.0 0.2 reduce-scatter.12.cloned.1.call-start
  222.2 0.5 copy-done.4
  222.7 0.2 copy-done.5
  222.9 0.9 convolution_convert_fusion.3
  223.9 0.0 reduce-scatter.12.cloned.1.call-update
  223.9 0.0 reduce-scatter.8.cloned.1.call-start
  223.9 74.9 %all-reduce.5.cloned.1.call-done = bf16[30,256,256]{2,1,0:T(8,128)(2,1)} async-done(((bf16[30,256,256]{2,1,0:T(8,128)(2,1)}), bf16[30,256,256]{2,1,0:T(8,128)(2,1)}) %all-reduce.5.cloned.1.call-update) | async-done | bytes 3932176 | tf_op jit(solution)/shard_map/psum | solution.py:15
  298.8 0.0 copy-done.1
  298.8 5.2 fusion.8
  304.0 0.0 copy-start.6
  304.0 3.8 fusion.15
  307.8 1.2 copy.18
  309.0 0.0 reduce-scatter.8.cloned.1.call-update
  309.1 24.8 %reduce-scatter.12.cloned.1.call-done = bf16[128,128]{1,0:T(8,128)(2,1)} async-done(((bf16[1024,128]{1,0:T(8,128)(2,1)}), bf16[128,128]{1,0:T(8,128)(2,1)}) %reduce-scatter.12.cloned.1.call-update) | async-done | bytes 32784
  333.9 0.9 copy.24
  334.8 219.9 %reduce-scatter.8.cloned.1.call-done = bf16[128,128]{1,0:T(8,128)(2,1)} async-done(((bf16[4096,128]{1,0:T(8,128)(2,1)}), bf16[128,128]{1,0:T(8,128)(2,1)}) %reduce-scatter.8.cloned.1.call-update) | async-done | bytes 32784 | tf_op jit(solution)/shard_map/reduce_scatter | solution.py:83
  554.7 0.0 copy-done.6
  554.7 1.6 fusion.18
  (2 shorter events, 0.0 us)
Async XLA Ops:
  7.2 89.5 %copy-start = (bf16[1024,128]{1,0:T(8,128)(2,1)S(1)}, bf16[1024,128]{1,0:T(8,128)(2,1)}, u32[]{:S(2)}) copy-start(bf16[1024,128]{1,0:T(8,128)(2,1)} %param.14) | copy-start | bytes 786436
  7.2 82.6 %all-gather.2.cloned.1.call-start = ((), (), s32[]{:S(2)}) async-start(), calls=%async_computation.3 | async-start | bytes 1081344 | tf_op jit(solution)/shard_map/all_gather | solution.py:52
  7.9 160.6 %all-reduce.3.cloned.1.call-start = ((), (), s32[]{:S(2)}) async-start(), calls=%async_computation.4 | async-start | bytes 7864320 | tf_op jit(solution)/shard_map/psum | solution.py:15
  96.5 1.0 copy-start.2
  96.6 114.1 %reduce-scatter.10.cloned.1.call-start = ((), (), s32[]{:S(2)}) async-start(), calls=%async_computation.7 | async-start | bytes 4718592
  100.8 198.0 %all-reduce.5.cloned.1.call-start = ((), (), s32[]{:S(2)}) async-start(), calls=%async_computation.5 | async-start | bytes 7864320 | tf_op jit(solution)/shard_map/psum | solution.py:15
  173.3 39.4 %copy-start.7 = (f32[128,128]{1,0:T(8,128)S(1)}, f32[128,128]{1,0:T(8,128)}, u32[]{:S(2)}) copy-start(f32[128,128]{1,0:T(8,128)} %param.16) | copy-start | bytes 196612
  215.2 6.8 %copy-start.3 = (bf16[2048,128]{1,0:T(8,128)(2,1)}, bf16[2048,128]{1,0:T(8,128)(2,1)S(1)}, u32[]{:S(2)}) copy-start(bf16[2048,128]{1,0:T(8,128)(2,1)S(1)} %fusion.14) | copy-start | bytes 1572868
  222.0 0.8 copy-start.4
  222.0 1.0 copy-start.5
  222.0 76.9 %copy-start.1 = (bf16[30,256,128]{2,1,0:T(8,128)(2,1)S(1)}, bf16[30,256,128]{2,1,0:T(8,128)(2,1)}, u32[]{:S(2)}) copy-start(bf16[30,256,128]{2,1,0:T(8,128)(2,1)} %gather_fusion.2) | copy-start | bytes 5898244
  222.0 111.9 %reduce-scatter.12.cloned.1.call-start = ((), (), s32[]{:S(2)}) async-start(), calls=%async_computation.8 | async-start | bytes 294912
  223.9 330.8 %reduce-scatter.8.cloned.1.call-start = ((), (), s32[]{:S(2)}) async-start(), calls=%async_computation.6 | async-start | bytes 1081344 | tf_op jit(solution)/shard_map/reduce_scatter | solution.py:83
  304.0 250.7 %copy-start.6 = (f32[128,128]{1,0:T(8,128)S(1)}, f32[128,128]{1,0:T(8,128)}, u32[]{:S(2)}) copy-start(f32[128,128]{1,0:T(8,128)} %param.17) | copy-start | bytes 196612
Sparse Core Ops, SparseCore 0:
  10.6 79.1 all-gather.1
  96.7 71.8 all-reduce.2
  171.1 39.5 reduce-scatter.9
  222.1 76.6 all-reduce.4
  301.2 32.6 reduce-scatter.11
  338.1 216.6 reduce-scatter.7
where the time goes:
time: 564 us; the launch traced here: 563 us
  waiting for transfers between devices  498 us (88%)
  matrix products  34.7 us (6%)
  between operations  14.9 us (3%)
  local copies, waits for them, and re-layouts  14.5 us (3%)
    reduce_scatter x1, waiting for transfers between devices, local(): lax.psum_scatter(item_sums.astype(jnp.bfloat16), 'users', scatter_dimensi...  220 us
    psum x2, waiting for transfers between devices, predict(): lax.psum(partial_value.astype(jnp.bfloat16), 'dims').astype(jnp.float32)  142 us
    all_gather x1, waiting for transfers between devices, local(): item_block = lax.all_gather(item_factors, 'users', axis=0, tiled=True)  77.9 us
    unnamed x8, waiting for transfers between devices  58.1 us
  transfers between devices with their start and end apart: 6, of which 6 were waited for; matrix products, arithmetic and copies ran while one was open for 5% of the time, Pallas kernels for 0%

commit v1 on v0

v1 whole, which is shorter than its diff:
```python
import functools

import jax
import jax.numpy as jnp
from jax import lax
from jax.experimental import pallas as pl
from jax.experimental.pallas import tpu as pltpu
from jax.sharding import PartitionSpec as P

UNOBSERVED = 256.0
REGULAR = 2.0
HIGHEST = lax.Precision.HIGHEST
MESH = pl.DeviceIdType.MESH
NY = 4
PARTS = 4
SEMS = 144


class Net:
    def __init__(self, send_sem, recv_sem):
        self.send_sem = send_sem
        self.recv_sem = recv_sem
        self.used = 0
        self.started = []

    def slot(self):
        self.used += 1
        return self.used - 1

    def push(self, index, source, target, device):
        copy = pltpu.make_async_remote_copy(
            src_ref=source,
            dst_ref=target,
            send_sem=self.send_sem.at[index],
            recv_sem=self.recv_sem.at[index],
            device_id=device,
            device_id_type=MESH,
        )
        copy.start()
        self.started.append(copy)

    def land(self, index, target, device):
        pltpu.make_async_remote_copy(
            src_ref=target,
            dst_ref=target,
            send_sem=self.send_sem.at[index],
            recv_sem=self.recv_sem.at[index],
            device_id=device,
            device_id_type=MESH,
        ).wait_recv()

    def drain(self):
        for copy in self.started:
            copy.wait_send()
        self.started = []


class Ring:
    def __init__(self, net, size, place, to, piece):
        self.net, self.size, self.place, self.to, self.piece = net, size, place, to, piece
        self.slots = {}
        for distance in range(1, size // 2 + 1):
            self.slots[distance] = (net.slot(), net.slot())

    def steps(self):
        return self.size // 2

    def halves(self, distance):
        return (0, 1) if 2 * distance == self.size else (None, None)

    def send(self, distance):
        if distance > self.steps():
            return
        for index, step, half in zip(self.slots[distance], (1, -1), self.halves(distance)):
            chunk = lax.rem(self.place - step * (distance - 1) + self.size, self.size)
            view = self.piece(chunk, half)
            self.net.push(index, view, view, self.to(step))

    def recv(self, distance):
        if distance > self.steps():
            return []
        came = []
        for index, step, half in zip(self.slots[distance], (1, -1), self.halves(distance)):
            chunk = lax.rem(self.place - step * distance + self.size, self.size)
            self.net.land(index, self.piece(chunk, half), self.to(step))
            came.append((chunk, half))
        return came


class Sibling:
    def __init__(self, net, core, device):
        self.net, self.core, self.device = net, core, device
        self.due = []

    def hand(self, piece):
        index = self.net.slot()
        view = piece(self.core)
        self.net.push(index, view, view, self.device)
        self.due.append((index, piece))

    def collect(self):
        for index, piece in self.due:
            self.net.land(index, piece(1 - self.core), self.device)
        self.due = []


def kernel(
    nx, nz, meta, u_hbm, i_hbm, r_hbm, ig, ug, ui, ii, unew_out, inew_out,
    users, items, news, ratings, errors, sums, running, coupled, icoupled,
    qs, ra, sa, ta, rb, sb, tb, send_sem, recv_sem, local_sem,
):
    ny = NY
    u = lax.axis_index("users")
    c = lax.axis_index("dims")
    y, z = lax.div(u, nz), lax.rem(u, nz)
    x, k = lax.div(c, 2), lax.rem(c, 2)

    def device(xx, kk, yy, zz):
        return (yy * nz + zz, xx * 2 + kk)

    def along_x(step):
        return device(lax.rem(x + step + nx, nx), k, y, z)

    def along_y(step):
        return device(x, k, lax.rem(y + step + ny, ny), z)

    def along_z(step):
        return device(x, k, y, lax.rem(z + step + nz, nz))

    other_core = device(x, 1 - k, y, z)
    row_tiles, tile, width = users.shape[2:]
    slots = ratings.shape[0]
    panels = ny * nz // 2

    own = [
        pltpu.make_async_copy(i_hbm, items.at[k, x, y, z], local_sem.at[0]),
        pltpu.make_async_copy(u_hbm, users.at[k, x], local_sem.at[1]),
        pltpu.make_async_copy(r_hbm, ratings, local_sem.at[2]),
    ]
    for copy in own:
        copy.start()

    barrier = pltpu.get_barrier_semaphore()
    peers = [along_x(s) for s in range(1, nx)]
    peers += [along_y(s) for s in range(1, ny)]
    peers += [along_z(s) for s in range(1, nz)]
    peers += [other_core]
    for peer in peers:
        pl.semaphore_signal(barrier, inc=1, device_id=peer, device_id_type=MESH)
    pl.semaphore_wait(barrier, len(peers))

    net = Net(send_sem, recv_sem)
    sibling = Sibling(net, k, other_core)
    own[0].wait()
    own[1].wait()

    first = [net.slot() for _ in range(1, nx)]
    for index, step in zip(first, range(1, nx)):
        view = items.at[k, x, y, z]
        net.push(index, view, view, along_x(step))

    half_rows = row_tiles // 2

    def user_piece(table):
        def piece(chunk, half, kk=None):
            kk = k if kk is None else kk
            if half is None:
                return table.at[kk, chunk]
            return table.at[kk, chunk, pl.ds(half * half_rows, half_rows)]

        return piece

    xu = Ring(net, nx, x, along_x, user_piece(users))
    xu.send(1)
    sibling.hand(lambda kk: users.at[kk, x])
    for index, step in zip(first, range(1, nx)):
        source = lax.rem(x - step + nx, nx)
        net.land(index, items.at[k, source, y, z], along_x(step))

    hx = nx // 2

    def span(part, half):
        if half is None or hx < 2:
            return pl.ds(part * hx, hx)
        return pl.ds(part * hx + half * (hx // 2), hx // 2)

    def rows_of(half):
        size = items.shape[4]
        if half is None or hx >= 2:
            return pl.ds(0, size)
        return pl.ds(half * (size // 2), size // 2)

    ay = Ring(net, ny, y, along_y, lambda n, h, kk=None: items.at[k if kk is None else kk, span(0, h), n, z, rows_of(h)])
    bz = Ring(net, nz, z, along_z, lambda n, h, kk=None: items.at[k if kk is None else kk, span(1, h), y, n, rows_of(h)])
    az = Ring(net, nz, z, along_z, lambda n, h, kk=None: items.at[k if kk is None else kk, span(0, h), :, n, rows_of(h)])
    by = Ring(net, ny, y, along_y, lambda n, h, kk=None: items.at[k if kk is None else kk, span(1, h), n, :, rows_of(h)])

    def pass_on(ring, came):
        for chunk, half in came:
            sibling.hand(functools.partial(lambda kk, r, n, h: r.piece(n, h, kk), r=ring, n=chunk, h=half))

    ay.send(1)
    bz.send(1)
    for step in range(1, max(ay.steps(), bz.steps()) + 1):
        ay.recv(step)
        ay.send(step + 1)
        if step == ay.steps():
            az.send(1)
            sibling.hand(lambda kk: items.at[kk, span(0, None), :, z])
        bz.recv(step)
        bz.send(step + 1)
    if ay.steps() == 0:
        az.send(1)
        sibling.hand(lambda kk: items.at[kk, span(0, None), :, z])
    by.send(1)
    sibling.hand(lambda kk: items.at[kk, span(1, None), y, :])
    xu_step = 1
    for step in range(1, max(az.steps(), by.steps()) + 1):
        came = az.recv(step)
        az.send(step + 1)
        pass_on(az, came)
        if step >= 2 or az.steps() < 2:
            came = xu.recv(xu_step)
            xu.send(xu_step + 1)
            pass_on(xu, came)
            xu_step += 1
            came = by.recv(step - 1 if az.steps() >= 2 else step)
            by.send(step if az.steps() >= 2 else step + 1)
            pass_on(by, came)
    while xu_step <= xu.steps():
        pass_on(xu, xu.recv(xu_step))
        xu.send(xu_step + 1)
        xu_step += 1
    for step in range(max(az.steps(), 1), by.steps() + 1):
        if az.steps() >= 2:
            pass_on(by, by.recv(step))
    sibling.collect()
    own[2].wait()

    def whole_rank(table, row):
        return jnp.concatenate([table[kk, xx, row] for xx in range(nx) for kk in range(2)], axis=1)

    def panel_block(kk, xx, py, pz):
        return items[kk, xx, py, pl.ds(pz, 2)].reshape(tile, width)

    def error_tile(table, i):
        row, py, pz = meta[1, i], meta[2, i], meta[3, i]
        panel = jnp.concatenate([panel_block(kk, xx, py, pz) for xx in range(nx) for kk in range(2)], axis=1)
        prediction = lax.dot_general(
            whole_rank(table, row), panel, (((1,), (1,)), ((), ())), preferred_element_type=jnp.float32
        )
        live = meta[4, i].astype(jnp.float32)
        return (live * (ratings[meta[0, i]].astype(jnp.float32) - prediction)).astype(jnp.bfloat16)

    @pl.loop(0, row_tiles)
    def _(r):
        coupled[r] = jnp.dot(whole_rank(users, r), ig[...], preferred_element_type=jnp.float32)

    mine = jnp.concatenate([items[kk, xx, y, z] for xx in range(nx) for kk in range(2)], axis=1)
    icoupled[...] = jnp.dot(mine, ug[...], preferred_element_type=jnp.float32)

    running[...] = jnp.zeros_like(running)

    @pl.loop(0, slots)
    def _(i):
        error = error_tile(users, i)
        added = jnp.dot(error, panel_block(k, x, meta[2, i], meta[3, i]), preferred_element_type=jnp.float32)
        total = running[...] * meta[5, i].astype(jnp.float32) + added
        running[...] = total
        sums[i] = total

    def newton(factors, gradient, inverse):
        update = jnp.dot(gradient, inverse, precision=HIGHEST, preferred_element_type=jnp.float32)
        return (factors + update).astype(jnp.bfloat16)

    per = row_tiles // PARTS
    rings = []
    out_copies = []
    for part in range(PARTS):

        @pl.loop(part * per, (part + 1) * per)
        def _(r):
            observed = sums[meta[9, r]] * meta[10, r].astype(jnp.float32)
            factors = users[k, x, r].astype(jnp.float32)
            gradient = observed - UNOBSERVED * coupled[r] - REGULAR * factors
            news[k, x, r] = newton(factors, gradient, ui[...])

        def piece(chunk, half, kk=None, part=part):
            kk = k if kk is None else kk
            if half is None:
                return news.at[kk, chunk, pl.ds(part * per, per)]
            return news.at[kk, chunk, pl.ds(part * per, per), pl.ds(half * (tile // 2), tile // 2)]

        ring = Ring(net, nx, x, along_x, piece)
        ring.send(1)
        sibling.hand(functools.partial(lambda kk, f: f(x, None, kk), f=piece))
        rings.append(ring)
        copy = pltpu.make_async_copy(
            news.at[k, x, pl.ds(part * per, per)], unew_out.at[pl.ds(part * per, per)], local_sem.at[3 + part]
        )
        copy.start()
        out_copies.append(copy)
    for step in range(1, nx // 2 + 1):
        for ring in rings:
            came = ring.recv(step)
            ring.send(step + 1)
            pass_on(ring, came)
    sibling.collect()

    @pl.loop(0, slots)
    def _(i):
        errors[i] = error_tile(news, i)

    running[...] = jnp.zeros_like(running)

    @pl.loop(0, slots)
    def _(i):
        added = lax.dot_general(
            errors[meta[6, i]],
            news[k, x, meta[7, i]],
            (((0,), (0,)), ((), ())),
            preferred_element_type=jnp.float32,
        )
        total = running[...] * meta[8, i].astype(jnp.float32) + added
        running[...] = total
        sums[i] = total

    owner_rows = items.shape[4]

    @pl.loop(0, panels)
    def _(p):
        panel = sums[meta[11, p]] * meta[12, p].astype(jnp.float32)
        pair = panel.astype(jnp.bfloat16).reshape(2, owner_rows, width)
        qs[lax.div(p, nz // 2), pl.ds(2 * lax.rem(p, nz // 2), 2)] = pair

    na = ra.shape[2]
    a_rows, b_rows = pl.ds(0, na), pl.ds(na, owner_rows - na)
    b_slots = [net.slot() for _ in range(1, ny)]
    a_slots = [net.slot() for _ in range(1, nz)]
    for step in range(1, ny):
        to = lax.rem(y + step, ny)
        net.push(b_slots[step - 1], qs.at[to, :, b_rows], rb.at[step - 1], along_y(step))
    for step in range(1, nz):
        to = lax.rem(z + step, nz)
        net.push(a_slots[step - 1], qs.at[:, to, a_rows], ra.at[step - 1], along_z(step))
    for step in range(1, nz):
        net.land(a_slots[step - 1], ra.at[step - 1], along_z(step))
    total = qs[:, z, a_rows].astype(jnp.float32)
    for step in range(1, nz):
        total = total + ra[step - 1].astype(jnp.float32)
    sa[...] = total.astype(jnp.bfloat16)
    c_slots = [net.slot() for _ in range(1, ny)]
    for step in range(1, ny):
        to = lax.rem(y + step, ny)
        net.push(c_slots[step - 1], sa.at[to], ta.at[step - 1], along_y(step))
    for step in range(1, ny):
        net.land(b_slots[step - 1], rb.at[step - 1], along_y(step))
    total = qs[y, :, b_rows].astype(jnp.float32)
    for step in range(1, ny):
        total = total + rb[step - 1].astype(jnp.float32)
    sb[...] = total.astype(jnp.bfloat16)
    d_slots = [net.slot() for _ in range(1, nz)]
    for step in range(1, nz):
        to = lax.rem(z + step, nz)
        net.push(d_slots[step - 1], sb.at[to], tb.at[step - 1], along_z(step))
    for step in range(1, ny):
        net.land(c_slots[step - 1], ta.at[step - 1], along_y(step))
    total_a = sa[y].astype(jnp.float32)
    for step in range(1, ny):
        total_a = total_a + ta[step - 1].astype(jnp.float32)
    for step in range(1, nz):
        net.land(d_slots[step - 1], tb.at[step - 1], along_z(step))
    total_b = sb[z].astype(jnp.float32)
    for step in range(1, nz):
        total_b = total_b + tb[step - 1].astype(jnp.float32)
    observed = jnp.concatenate([total_a, total_b], axis=0)
    factors = items[k, x, y, z].astype(jnp.float32)
    gradient = observed - UNOBSERVED * icoupled[...] - REGULAR * factors
    inew_out[...] = newton(factors, gradient, ii[...])
    for copy in out_copies:
        copy.wait()
    net.drain()


def lookup(tile_coords, tile_count, row_tiles, panel_count, nz):
    count = tile_coords.shape[0]
    row, panel = tile_coords[:, 0], tile_coords[:, 1]
    slot = lax.iota(jnp.int32, count)
    live = (slot < tile_count[0]).astype(jnp.int32)

    def rank_of(value):
        key = value * count + slot
        return jnp.sum((key[None, :] < key[:, None]).astype(jnp.int32), axis=1)

    def sort_by(rank, value):
        return jnp.sum(jnp.where(rank[None, :] == slot[:, None], value[None, :], 0), axis=1)

    def same(value):
        return jnp.concatenate([jnp.zeros((1,), jnp.int32), (value[1:] == value[:-1]).astype(jnp.int32)])

    def last(value, size):
        ids = lax.iota(jnp.int32, size)[:, None]
        upto = jnp.sum((value[None, :] <= ids).astype(jnp.int32), axis=1)
        has = jnp.any(value[None, :] == ids, axis=1).astype(jnp.int32)
        return jnp.maximum(upto - 1, 0), has

    by_row, by_panel = rank_of(row), rank_of(panel)
    sorted_row, sorted_panel = sort_by(by_row, row), sort_by(by_row, panel)
    last_row, has_row = last(row, row_tiles)
    last_panel, has_panel = last(panel, panel_count)
    lines = [
        sort_by(by_row, slot),
        sorted_row,
        sorted_panel // (nz // 2),
        2 * (sorted_panel % (nz // 2)),
        sort_by(by_row, live),
        same(sorted_row),
        sort_by(by_panel, by_row),
        sort_by(by_panel, row),
        same(sort_by(by_panel, panel)),
        last_row,
        has_row,
        last_panel,
        has_panel,
    ]
    wide = max(count, row_tiles, panel_count)
    return jnp.stack([jnp.pad(line, (0, wide - line.shape[0])) for line in lines])


def local(nx, nz, user_factors, item_factors, ratings, tile_coords, tile_count, item_gram, user_gram, user_inverse, item_inverse):
    user_rows, width = user_factors.shape
    owner_rows = item_factors.shape[0]
    slots, tile, _ = ratings.shape
    row_tiles = user_rows // tile
    panel_count = NY * nz * owner_rows // tile
    meta = lookup(tile_coords, tile_count, row_tiles, panel_count, nz)
    na = owner_rows // 4
    nb = owner_rows - na
    bf16, f32 = jnp.bfloat16, jnp.float32
    vmem = pl.BlockSpec(memory_space=pltpu.VMEM)
    hbm = pl.BlockSpec(memory_space=pl.ANY)
    user_new, item_new = pl.pallas_call(
        functools.partial(kernel, nx, nz),
        out_shape=(
            jax.ShapeDtypeStruct((row_tiles, tile, width), bf16),
            jax.ShapeDtypeStruct((owner_rows, width), bf16),
        ),
        in_specs=[pl.BlockSpec(memory_space=pltpu.SMEM), hbm, hbm, hbm, vmem, vmem, vmem, vmem],
        out_specs=(hbm, vmem),
        scratch_shapes=[
            pltpu.VMEM((2, nx, row_tiles, tile, width), bf16),
            pltpu.VMEM((2, nx, NY, nz, owner_rows, width), bf16),
            pltpu.VMEM((2, nx, row_tiles, tile, width), bf16),
            pltpu.VMEM((slots, tile, tile), bf16),
            pltpu.VMEM((slots, tile, tile), bf16),
            pltpu.VMEM((slots, tile, width), f32),
            pltpu.VMEM((tile, width), f32),
            pltpu.VMEM((row_tiles, tile, width), f32),
            pltpu.VMEM((owner_rows, width), f32),
            pltpu.VMEM((NY, nz, owner_rows, width), bf16),
            pltpu.VMEM((nz - 1, NY, na, width), bf16),
            pltpu.VMEM((NY, na, width), bf16),
            pltpu.VMEM((max(NY - 1, 1), na, width), bf16),
            pltpu.VMEM((max(NY - 1, 1), nz, nb, width), bf16),
            pltpu.VMEM((nz, nb, width), bf16),
            pltpu.VMEM((nz - 1, nb, width), bf16),
            pltpu.SemaphoreType.DMA((SEMS,)),
            pltpu.SemaphoreType.DMA((SEMS,)),
            pltpu.SemaphoreType.DMA((3 + PARTS,)),
        ],
        compiler_params=pltpu.CompilerParams(
            collective_id=0, has_side_effects=True, vmem_limit_bytes=56 * 1024 * 1024
        ),
    )(
        meta,
        user_factors.reshape(row_tiles, tile, width),
        item_factors,
        ratings,
        item_gram,
        user_gram,
        user_inverse,
        item_inverse,
    )
    return user_new.reshape(user_rows, width), item_new


def solution(mesh):
    placed = (
        P("users", "dims"),
        P("users", "dims"),
        P("users", None, None),
        P("users", None),
        P("users"),
        P(None, "dims"),
        P(None, "dims"),
        P("dims", None),
        P("dims", None),
    )
    return jax.shard_map(
        functools.partial(local, mesh.shape["dims"] // 2, mesh.shape["users"] // NY),
        mesh=mesh,
        in_specs=placed,
        out_specs=(P("users", "dims"), P("users", "dims")),
        check_vma=False,
    )
```

time: 564 us -> 141 us (0.25)
  waiting for transfers between devices: 498 us -> 0 us
  Pallas kernels: 0 us -> 132 us
  matrix products: 34.7 us -> 0 us
  between operations: 14.9 us -> 1.32 us
  local copies, waits for them, and re-layouts: 14.5 us -> 4.47 us
    reduce_scatter x1 -> x0, waiting for transfers between devices: 220 us -> none  [local(): lax.psum_scatter(item_sums.astype(jnp.bfloat16), 'users', scatter_dimensi...]
    psum x2 -> x0, waiting for transfers between devices: 142 us -> none  [predict(): lax.psum(partial_value.astype(jnp.bfloat16), 'dims').astype(jnp.float32)]
    pallas_call x0 -> x1, Pallas kernels: none -> 132 us  [local(): pl.pallas_call(functools.partial(kernel, nx, nz), out_shape=(jax.ShapeDty...]
    all_gather x1 -> x0, waiting for transfers between devices: 77.9 us -> none  [local(): item_block = lax.all_gather(item_factors, 'users', axis=0, tiled=True)]
    unnamed x8 -> x0, waiting for transfers between devices: 58.1 us -> none
    dot_general x10 -> x0, matrix products: 34.7 us -> none  [the longest x2 9.22 us: predict(): jnp.einsum('sik,sjk->sij', user_tiles, item_tiles, preferred_element_type...]
    gather x3 -> x0, local copies, waits for them, and re-layouts: 7.48 us -> none  [the longest x1 3.16 us: local(): user_factors.reshape(row_tiles, tile_size, block_width)[row_index]]
  transfers between devices with their start and end apart: 6 -> 0, of which waited for: 6 -> 0; matrix products, arithmetic and copies ran while one was open for 5% -> 0% of each run, Pallas kernels for 0% -> 0%
where the time goes in v1:
time: 141 us
  Pallas kernels  132 us (94%)
  local copies, waits for them, and re-layouts  4.47 us (3%)
  other arithmetic  2.73 us (2%)
    pallas_call x1, Pallas kernels, local(): pl.pallas_call(functools.partial(kernel, nx, nz), out_shape=(jax.ShapeDty...  132 us
    unnamed x2, local copies, waits for them, and re-layouts  3.24 us

profile of v1, /device:TPU:2, one launch (start us, length us, event | category | flops | bytes accessed | tf_op | source)
XLA Modules:
  0.0 140.7 jit_solution(4902060868712660469)
XLA Ops:
  1.3 0.8 iota_add_fusion.1
  2.0 0.8 slice_bitcast_fusion.1
  2.8 0.2 convert_reduce_fusion
  3.0 0.1 convert_reduce_fusion.3
  3.1 0.1 fusion.1
  3.2 0.1 convert_reduce_fusion.2
  3.4 0.1 fusion
  3.5 0.2 select_reduce_fusion
  3.7 0.1 slice_compare_fusion
  3.8 0.1 fusion.7
  3.9 0.1 slice_compare_fusion.1
  4.0 0.1 fusion.8
  4.0 1.2 stack.65.meta
  5.3 132.1 %shard_map.104 = (bf16[8,256,128]{2,1,0:T(8,128)(2,1)}, bf16[128,128]{1,0:T(8,128)(2,1)}) custom-call(s32[13,30]{1,0:T(8,128)} %stack.65.meta, bf16[8,256,128]{2,1,0:T(8,128)(2,1)} %bitcast.48, bf16[128,128]{1,0:T(8,128)(2,1)} %i_hbm.1, bf16[30,256,256]{2,1,0:T(8,128)(2,1)} %r_hbm.1, bf16[1024,128]{1,0:T(8,128)(2,1)} %ig.1, bf16[1024,128]{1,0:T(8,128)(2,1)} %ug.1, ...), custom_call_target="tpu_custom_call" | custom-call | tf_op jit(solution)/shard_map/pallas_call | solution.py:442
  137.4 1.9 %copy.14 = bf16[2048,128]{1,0:T(8,128)(2,1)} copy(bf16[2048,128]{1,0:T(8,128)(2,1)} %bitcast.49) | data formatting | bytes 1048576
  139.3 1.4 copy.15
  (6 shorter events, 0.0 us)

commit v2 on v1

--- a/solution.py
+++ b/solution.py
@@ -13,7 +13,8 @@
 MESH = pl.DeviceIdType.MESH
 NY = 4
 PARTS = 4
-SEMS = 144
+SEMS = 240
+UNROLL = 5
 
 
 class Net:
@@ -90,18 +91,21 @@
 class Sibling:
     def __init__(self, net, core, device):
         self.net, self.core, self.device = net, core, device
-        self.due = []
+        self.due = {}
 
     def hand(self, piece):
         index = self.net.slot()
         view = piece(self.core)
         self.net.push(index, view, view, self.device)
-        self.due.append((index, piece))
+        self.due[index] = piece
+        return index
+
+    def wait(self, index):
+        self.net.land(index, self.due.pop(index)(1 - self.core), self.device)
 
     def collect(self):
-        for index, piece in self.due:
-            self.net.land(index, piece(1 - self.core), self.device)
-        self.due = []
+        for index in list(self.due):
+            self.wait(index)
 
 
 def kernel(
@@ -172,7 +176,7 @@
 
     xu = Ring(net, nx, x, along_x, user_piece(users))
     xu.send(1)
-    sibling.hand(lambda kk: users.at[kk, x])
+    own_users = sibling.hand(lambda kk: users.at[kk, x])
     for index, step in zip(first, range(1, nx)):
         source = lax.rem(x - step + nx, nx)
         net.land(index, items.at[k, source, y, z], along_x(step))
@@ -190,50 +194,98 @@
             return pl.ds(0, size)
         return pl.ds(half * (size // 2), size // 2)
 
+    def pass_on(ring, came):
+        return [sibling.hand(functools.partial(ring.piece, chunk, half)) for chunk, half in came]
+
+    active = []
+
+    def start(ring, arrived):
+        ring.send(1)
+        active.append([ring, 1, arrived])
+
+    def wave():
+        for entry in list(active):
+            ring, step, arrived = entry
+            if step <= ring.steps():
+                came = ring.recv(step)
+                ring.send(step + 1)
+                arrived(step, came)
+                entry[1] += 1
+
+    def second_z(yy, is_last):
+        def arrived(step, came):
+            for n, h in came if is_last else []:
+                sibling.hand(lambda kk, n=n, h=h: items.at[kk, span(0, h), :, n, rows_of(h)])
+
+        start(Ring(net, nz, z, along_z, lambda n, h, kk=None: items.at[k if kk is None else kk, span(0, h), yy, n, rows_of(h)]), arrived)
+
+    def second_y(zz, is_last):
+        def arrived(step, came):
+            for n, h in came if is_last else []:
+                sibling.hand(lambda kk, n=n, h=h: items.at[kk, span(1, h), n, :, rows_of(h)])
+
+        start(Ring(net, ny, y, along_y, lambda n, h, kk=None: items.at[k if kk is None else kk, span(1, h), n, zz, rows_of(h)]), arrived)
+
+    def first_y(step, came):
+        at_end = step == ay.steps()
+        for chunk in [came[0][0]] if at_end else [n for n, _ in came]:
+            second_z(chunk, at_end)
+        if at_end:
+            sibling.hand(lambda kk: items.at[kk, span(0, None), :, z])
+
+    def first_z(step, came):
+        at_end = step == bz.steps()
+        for chunk in [came[0][0]] if at_end else [n for n, _ in came]:
+            second_y(chunk, at_end)
+        if at_end:
+            sibling.hand(lambda kk: items.at[kk, span(1, None), y, :])
+
+    def couple(chunk, begin):
+        @pl.loop(0, row_tiles)
+        def _(r):
+            pair = jnp.concatenate([users[0, chunk, r], users[1, chunk, r]], axis=1)
+            product = jnp.dot(pair, ig[chunk], preferred_element_type=jnp.float32)
+            coupled[r] = product if begin else coupled[r] + product
+
     ay = Ring(net, ny, y, along_y, lambda n, h, kk=None: items.at[k if kk is None else kk, span(0, h), n, z, rows_of(h)])
     bz = Ring(net, nz, z, along_z, lambda n, h, kk=None: items.at[k if kk is None else kk, span(1, h), y, n, rows_of(h)])
-    az = Ring(net, nz, z, along_z, lambda n, h, kk=None: items.at[k if kk is None else kk, span(0, h), :, n, rows_of(h)])
-    by = Ring(net, ny, y, along_y, lambda n, h, kk=None: items.at[k if kk is None else kk, span(1, h), n, :, rows_of(h)])
-
-    def pass_on(ring, came):
-        for chunk, half in came:
-            sibling.hand(functools.partial(lambda kk, r, n, h: r.piece(n, h, kk), r=ring, n=chunk, h=half))
-
-    ay.send(1)
-    bz.send(1)
-    for step in range(1, max(ay.steps(), bz.steps()) + 1):
-        ay.recv(step)
-        ay.send(step + 1)
-        if step == ay.steps():
-            az.send(1)
-            sibling.hand(lambda kk: items.at[kk, span(0, None), :, z])
-        bz.recv(step)
-        bz.send(step + 1)
+    start(ay, first_y)
+    start(bz, first_z)
+    second_z(y, ay.steps() == 0)
+    second_y(z, bz.steps() == 0)
     if ay.steps() == 0:
-        az.send(1)
         sibling.hand(lambda kk: items.at[kk, span(0, None), :, z])
-    by.send(1)
-    sibling.hand(lambda kk: items.at[kk, span(1, None), y, :])
-    xu_step = 1
-    for step in range(1, max(az.steps(), by.steps()) + 1):
-        came = az.recv(step)
-        az.send(step + 1)
-        pass_on(az, came)
-        if step >= 2 or az.steps() < 2:
+    waves = ay.steps() + nz // 2
+    waves = max(waves, bz.steps() + ny // 2)
+    user_hands = []
+    met = xu_step = 0
+    for number in range(1, waves + 1):
+        wave()
+        if number == 2 or (number == waves and number < 2):
+            sibling.wait(own_users)
+            couple(x, True)
+        if number in (3, 5) and xu_step < xu.steps():
+            xu_step += 1
             came = xu.recv(xu_step)
             xu.send(xu_step + 1)
-            pass_on(xu, came)
-            xu_step += 1
-            came = by.recv(step - 1 if az.steps() >= 2 else step)
-            by.send(step if az.steps() >= 2 else step + 1)
-            pass_on(by, came)
-    while xu_step <= xu.steps():
-        pass_on(xu, xu.recv(xu_step))
+            user_hands.append((came, pass_on(xu, came)))
+        if number == 4 and user_hands and 2 < nx:
+            came, hands = user_hands[0]
+            for (chunk, _), hand in zip(came, hands):
+                sibling.wait(hand)
+                couple(chunk, False)
+            met = 1
+    while xu_step < xu.steps():
+        xu_step += 1
+        came = xu.recv(xu_step)
         xu.send(xu_step + 1)
-        xu_step += 1
-    for step in range(max(az.steps(), 1), by.steps() + 1):
-        if az.steps() >= 2:
-            pass_on(by, by.recv(step))
+        user_hands.append((came, pass_on(xu, came)))
+    for step, (came, hands) in enumerate(user_hands):
+        if step >= met:
+            for hand in hands:
+                sibling.wait(hand)
+            for chunk in [came[0][0]] if step == xu.steps() - 1 else [n for n, _ in came]:
+                couple(chunk, False)
     sibling.collect()
     own[2].wait()
 
@@ -252,16 +304,9 @@
         live = meta[4, i].astype(jnp.float32)
         return (live * (ratings[meta[0, i]].astype(jnp.float32) - prediction)).astype(jnp.bfloat16)
 
-    @pl.loop(0, row_tiles)
-    def _(r):
-        coupled[r] = jnp.dot(whole_rank(users, r), ig[...], preferred_element_type=jnp.float32)
-
-    mine = jnp.concatenate([items[kk, xx, y, z] for xx in range(nx) for kk in range(2)], axis=1)
-    icoupled[...] = jnp.dot(mine, ug[...], preferred_element_type=jnp.float32)
-
     running[...] = jnp.zeros_like(running)
 
-    @pl.loop(0, slots)
+    @pl.loop(0, slots, unroll=UNROLL)
     def _(i):
         error = error_tile(users, i)
         added = jnp.dot(error, panel_block(k, x, meta[2, i], meta[3, i]), preferred_element_type=jnp.float32)
@@ -293,13 +338,16 @@
 
         ring = Ring(net, nx, x, along_x, piece)
         ring.send(1)
-        sibling.hand(functools.partial(lambda kk, f: f(x, None, kk), f=piece))
+        sibling.hand(functools.partial(piece, x, None))
         rings.append(ring)
         copy = pltpu.make_async_copy(
             news.at[k, x, pl.ds(part * per, per)], unew_out.at[pl.ds(part * per, per)], local_sem.at[3 + part]
         )
         copy.start()
         out_copies.append(copy)
+    mine = jnp.concatenate([items[kk, xx, y, z] for xx in range(nx) for kk in range(2)], axis=1)
+    icoupled[...] = jnp.dot(mine, ug[...], preferred_element_type=jnp.float32)
+
     for step in range(1, nx // 2 + 1):
         for ring in rings:
             came = ring.recv(step)
@@ -307,13 +355,13 @@
             pass_on(ring, came)
     sibling.collect()
 
-    @pl.loop(0, slots)
+    @pl.loop(0, slots, unroll=UNROLL)
     def _(i):
         errors[i] = error_tile(news, i)
 
     running[...] = jnp.zeros_like(running)
 
-    @pl.loop(0, slots)
+    @pl.loop(0, slots, unroll=UNROLL)
     def _(i):
         added = lax.dot_general(
             errors[meta[6, i]],
@@ -476,7 +524,7 @@
         user_factors.reshape(row_tiles, tile, width),
         item_factors,
         ratings,
-        item_gram,
+        item_gram.reshape(nx, 2 * width, width),
         user_gram,
         user_inverse,
         item_inverse,

time: 141 us -> 121 us (0.86)
  Pallas kernels: 132 us -> 113 us
    pallas_call x1, Pallas kernels: 132 us -> 113 us  [local(): pl.pallas_call(functools.partial(kernel, nx, nz), out_shape=(jax.ShapeDty...]
where the time goes in v2:
time: 121 us
  Pallas kernels  113 us (93%)
  local copies, waits for them, and re-layouts  4.47 us (4%)
  other arithmetic  2.73 us (2%)
  between operations  1.32 us (1%)
    pallas_call x1, Pallas kernels, local(): pl.pallas_call(functools.partial(kernel, nx, nz), out_shape=(jax.ShapeDty...  113 us
    unnamed x2, local copies, waits for them, and re-layouts  3.24 us

profile of v2, /device:TPU:2, one launch (start us, length us, event | category | flops | bytes accessed | tf_op | source)
XLA Modules:
  0.0 121.1 jit_solution(16931176589781081532)
XLA Ops:
  1.3 0.8 iota_add_fusion.1
  2.0 0.8 slice_bitcast_fusion.1
  2.8 0.2 convert_reduce_fusion
  3.0 0.1 convert_reduce_fusion.3
  3.1 0.1 fusion.1
  3.2 0.1 convert_reduce_fusion.2
  3.4 0.1 fusion
  3.5 0.2 select_reduce_fusion
  3.7 0.1 slice_compare_fusion
  3.8 0.1 fusion.7
  3.9 0.1 slice_compare_fusion.1
  4.0 0.1 fusion.8
  4.0 1.2 %stack.65.meta = s32[13,30]{1,0:T(8,128)} concatenate(s32[1,30]{1,0:T(1,128)S(1)} %bitcast.56, s32[1,30]{1,0:T(1,128)S(1)} %bitcast.54, s32[1,30]{1,0:T(1,128)S(1)} %get-tuple-element.20, s32[1,30]{1,0:T(1,128)S(1)} %get-tuple-element.19, s32[1,30]{1,0:T(1,128)S(1)} %bitcast.53, s32[1,30]{1,0:T(1,128)S(1)} %fusion.8, s32[1,30]{1,0:T(1,128)S(1)} %bitcast.52, ...), dimensions={0} | concatenate | bytes 3120 | tf_op jit(solution)/shard_map/stack | solution.py:475
  5.3 112.6 %shard_map.104 = (bf16[8,256,128]{2,1,0:T(8,128)(2,1)}, bf16[128,128]{1,0:T(8,128)(2,1)}) custom-call(s32[13,30]{1,0:T(8,128)} %stack.65.meta, bf16[8,256,128]{2,1,0:T(8,128)(2,1)} %bitcast.49, bf16[128,128]{1,0:T(8,128)(2,1)} %i_hbm.1, bf16[30,256,256]{2,1,0:T(8,128)(2,1)} %r_hbm.1, bf16[4,256,128]{2,1,0:T(8,128)(2,1)} %bitcast.51, bf16[1024,128]{1,0:T(8,128)(2,1)} %ug.1, ...), custom_call_target="tpu_custom_call" | custom-call | tf_op jit(solution)/shard_map/pallas_call | solution.py:490
  117.9 1.9 %copy.14 = bf16[2048,128]{1,0:T(8,128)(2,1)} copy(bf16[2048,128]{1,0:T(8,128)(2,1)} %bitcast.50) | data formatting | bytes 1048576
  119.8 1.4 %copy.15 = bf16[128,128]{1,0:T(8,128)(2,1)} copy(bf16[128,128]{1,0:T(8,128)(2,1)} %get-tuple-element.30) | data formatting | bytes 65536
  (6 shorter events, 0.0 us)

commit v3 on v2

--- a/solution.py
+++ b/solution.py
@@ -88,6 +88,38 @@
         return came
 
 
+class Direct:
+    def __init__(self, net, size, place, to, piece):
+        self.net, self.size, self.place, self.to, self.piece = net, size, place, to, piece
+        near = [step for step in (1, -1, 2, -2) if abs(step) < size]
+        near = [step for n, step in enumerate(near) if step % size not in [e % size for e in near[:n]]]
+        self.plan = [[(net.slot(), 0, step, None) for step in near]] if near else []
+        if size == 8:
+            self.plan.append([(net.slot(), 2, 1, None), (net.slot(), -2, -1, None), (net.slot(), 2, 2, 0), (net.slot(), -2, -2, 1)])
+
+    def steps(self):
+        return len(self.plan)
+
+    def chunk(self, back):
+        return lax.rem(self.place - back + self.size, self.size)
+
+    def send(self, step):
+        if step > self.steps():
+            return
+        for index, back, jump, half in self.plan[step - 1]:
+            view = self.piece(self.chunk(back), half)
+            self.net.push(index, view, view, self.to(jump))
+
+    def recv(self, step):
+        came = []
+        for index, back, jump, half in self.plan[step - 1]:
+            chunk = self.chunk(back + jump)
+            self.net.land(index, self.piece(chunk, half), self.to(jump))
+            if half != 0:
+                came.append(chunk)
+        return came
+
+
 class Sibling:
     def __init__(self, net, core, device):
         self.net, self.core, self.device = net, core, device
@@ -181,64 +213,62 @@
         source = lax.rem(x - step + nx, nx)
         net.land(index, items.at[k, source, y, z], along_x(step))
 
-    hx = nx // 2
-
-    def span(part, half):
-        if half is None or hx < 2:
-            return pl.ds(part * hx, hx)
-        return pl.ds(part * hx + half * (hx // 2), hx // 2)
-
-    def rows_of(half):
-        size = items.shape[4]
-        if half is None or hx >= 2:
-            return pl.ds(0, size)
-        return pl.ds(half * (size // 2), size // 2)
+    owner_rows = items.shape[4]
+    split = owner_rows * 3 // 8 // 16 * 16
+
+    def blocks(half):
+        if half is None or nx < 2:
+            return pl.ds(0, nx)
+        return pl.ds(half * (nx // 2), nx // 2)
+
+    def rows_of(part, half):
+        low, size = (split, owner_rows - split) if part else (0, split)
+        if half is None or nx >= 2:
+            return pl.ds(low, size)
+        return pl.ds(low + half * (size // 2), size // 2)
+
+    def item_piece(part, yy, zz, half, kk=None):
+        return items.at[k if kk is None else kk, blocks(half), yy, zz, rows_of(part, half)]
 
     def pass_on(ring, came):
         return [sibling.hand(functools.partial(ring.piece, chunk, half)) for chunk, half in came]
 
     active = []
-
-    def start(ring, arrived):
+    whole = slice(None)
+
+    def start(order, ring, arrived):
         ring.send(1)
-        active.append([ring, 1, arrived])
+        active.append([order, ring, 1, arrived])
 
     def wave():
-        for entry in list(active):
-            ring, step, arrived = entry
+        for entry in sorted(active, key=lambda entry: entry[0]):
+            _, ring, step, arrived = entry
             if step <= ring.steps():
                 came = ring.recv(step)
                 ring.send(step + 1)
                 arrived(step, came)
-                entry[1] += 1
-
-    def second_z(yy, is_last):
-        def arrived(step, came):
-            for n, h in came if is_last else []:
-                sibling.hand(lambda kk, n=n, h=h: items.at[kk, span(0, h), :, n, rows_of(h)])
-
-        start(Ring(net, nz, z, along_z, lambda n, h, kk=None: items.at[k if kk is None else kk, span(0, h), yy, n, rows_of(h)]), arrived)
+                entry[2] += 1
+
+    def second_z(step, came):
+        if step == az.steps():
+            sibling.hand(functools.partial(item_piece, 0, whole, whole, None))
 
     def second_y(zz, is_last):
         def arrived(step, came):
             for n, h in came if is_last else []:
-                sibling.hand(lambda kk, n=n, h=h: items.at[kk, span(1, h), n, :, rows_of(h)])
-
-        start(Ring(net, ny, y, along_y, lambda n, h, kk=None: items.at[k if kk is None else kk, span(1, h), n, zz, rows_of(h)]), arrived)
+                sibling.hand(functools.partial(item_piece, 1, n, whole, h))
+
+        start(2, Ring(net, ny, y, along_y, lambda n, h: item_piece(1, n, zz, h)), arrived)
 
     def first_y(step, came):
-        at_end = step == ay.steps()
-        for chunk in [came[0][0]] if at_end else [n for n, _ in came]:
-            second_z(chunk, at_end)
-        if at_end:
-            sibling.hand(lambda kk: items.at[kk, span(0, None), :, z])
+        if step == ay.steps():
+            start(1, az, second_z)
 
     def first_z(step, came):
-        at_end = step == bz.steps()
-        for chunk in [came[0][0]] if at_end else [n for n, _ in came]:
-            second_y(chunk, at_end)
-        if at_end:
-            sibling.hand(lambda kk: items.at[kk, span(1, None), y, :])
+        for n, chunk in enumerate(came):
+            second_y(chunk, step == bz.steps() and n == len(came) - 1)
+        if step == bz.steps():
+            sibling.hand(functools.partial(item_piece, 1, y, whole, None))
 
     def couple(chunk, begin):
         @pl.loop(0, row_tiles)
@@ -247,29 +277,28 @@
             product = jnp.dot(pair, ig[chunk], preferred_element_type=jnp.float32)
             coupled[r] = product if begin else coupled[r] + product
 
-    ay = Ring(net, ny, y, along_y, lambda n, h, kk=None: items.at[k if kk is None else kk, span(0, h), n, z, rows_of(h)])
-    bz = Ring(net, nz, z, along_z, lambda n, h, kk=None: items.at[k if kk is None else kk, span(1, h), y, n, rows_of(h)])
-    start(ay, first_y)
-    start(bz, first_z)
-    second_z(y, ay.steps() == 0)
+    ay = Direct(net, ny, y, along_y, lambda n, h: item_piece(0, n, z, h))
+    bz = Direct(net, nz, z, along_z, lambda n, h: item_piece(1, y, n, h))
+    az = Ring(net, nz, z, along_z, lambda n, h: item_piece(0, whole, n, h))
+    start(0, ay, first_y)
+    start(0, bz, first_z)
     second_y(z, bz.steps() == 0)
     if ay.steps() == 0:
-        sibling.hand(lambda kk: items.at[kk, span(0, None), :, z])
-    waves = ay.steps() + nz // 2
-    waves = max(waves, bz.steps() + ny // 2)
+        start(1, az, second_z)
+    waves = max(ay.steps() + az.steps(), bz.steps() + ny // 2)
     user_hands = []
     met = xu_step = 0
     for number in range(1, waves + 1):
         wave()
-        if number == 2 or (number == waves and number < 2):
+        if number == 1:
             sibling.wait(own_users)
             couple(x, True)
-        if number in (3, 5) and xu_step < xu.steps():
+        if number in (2, 4) and xu_step < xu.steps():
             xu_step += 1
             came = xu.recv(xu_step)
             xu.send(xu_step + 1)
             user_hands.append((came, pass_on(xu, came)))
-        if number == 4 and user_hands and 2 < nx:
+        if number == 3 and user_hands and 2 < nx:
             came, hands = user_hands[0]
             for (chunk, _), hand in zip(came, hands):
                 sibling.wait(hand)
@@ -304,12 +333,16 @@
         live = meta[4, i].astype(jnp.float32)
         return (live * (ratings[meta[0, i]].astype(jnp.float32) - prediction)).astype(jnp.bfloat16)
 
-    running[...] = jnp.zeros_like(running)
-
     @pl.loop(0, slots, unroll=UNROLL)
     def _(i):
-        error = error_tile(users, i)
-        added = jnp.dot(error, panel_block(k, x, meta[2, i], meta[3, i]), preferred_element_type=jnp.float32)
+        errors[i] = error_tile(users, i)
+
+    running[...] = jnp.zeros_like(running)
+
+    @pl.loop(0, slots, unroll=UNROLL)
+    def _(i):
+        block = panel_block(k, x, meta[2, i], meta[3, i])
+        added = jnp.dot(errors[i], block, preferred_element_type=jnp.float32)
         total = running[...] * meta[5, i].astype(jnp.float32) + added
         running[...] = total
         sums[i] = total
@@ -372,8 +405,6 @@
         total = running[...] * meta[8, i].astype(jnp.float32) + added
         running[...] = total
         sums[i] = total
-
-    owner_rows = items.shape[4]
 
     @pl.loop(0, panels)
     def _(p):
@@ -482,7 +513,7 @@
     row_tiles = user_rows // tile
     panel_count = NY * nz * owner_rows // tile
     meta = lookup(tile_coords, tile_count, row_tiles, panel_count, nz)
-    na = owner_rows // 4
+    na = owner_rows * 3 // 8 // 16 * 16
     nb = owner_rows - na
     bf16, f32 = jnp.bfloat16, jnp.float32
     vmem = pl.BlockSpec(memory_space=pltpu.VMEM)

time: 121 us -> 114 us (0.942)
  Pallas kernels: 113 us -> 105 us
    pallas_call x1, Pallas kernels: 113 us -> 105 us  [local(): pl.pallas_call(functools.partial(kernel, nx, nz), out_shape=(jax.ShapeDty...]
where the time goes in v3:
time: 114 us; the launch traced here: 113 us
  Pallas kernels  105 us (92%)
  local copies, waits for them, and re-layouts  4.47 us (4%)
  other arithmetic  2.73 us (2%)
  between operations  1.32 us (1%)
    pallas_call x1, Pallas kernels, local(): pl.pallas_call(functools.partial(kernel, nx, nz), out_shape=(jax.ShapeDty...  105 us
    unnamed x2, local copies, waits for them, and re-layouts  3.24 us

profile of v3, /device:TPU:2, one launch (start us, length us, event | category | flops | bytes accessed | tf_op | source)
XLA Modules:
  0.0 113.5 jit_solution(5879754597147108052)
XLA Ops:
  1.3 0.8 iota_add_fusion.1
  2.0 0.8 slice_bitcast_fusion.1
  2.8 0.2 convert_reduce_fusion
  3.0 0.1 convert_reduce_fusion.3
  3.1 0.1 fusion.1
  3.2 0.1 convert_reduce_fusion.2
  3.4 0.1 fusion
  3.5 0.2 select_reduce_fusion
  3.7 0.1 slice_compare_fusion
  3.8 0.1 fusion.7
  3.9 0.1 slice_compare_fusion.1
  4.0 0.1 fusion.8
  4.0 1.2 %stack.65.meta = s32[13,30]{1,0:T(8,128)} concatenate(s32[1,30]{1,0:T(1,128)S(1)} %bitcast.56, s32[1,30]{1,0:T(1,128)S(1)} %bitcast.54, s32[1,30]{1,0:T(1,128)S(1)} %get-tuple-element.20, s32[1,30]{1,0:T(1,128)S(1)} %get-tuple-element.19, s32[1,30]{1,0:T(1,128)S(1)} %bitcast.53, s32[1,30]{1,0:T(1,128)S(1)} %fusion.8, s32[1,30]{1,0:T(1,128)S(1)} %bitcast.52, ...), dimensions={0} | concatenate | bytes 3120 | tf_op jit(solution)/shard_map/stack | solution.py:506
  5.3 105.0 %shard_map.104 = (bf16[8,256,128]{2,1,0:T(8,128)(2,1)}, bf16[128,128]{1,0:T(8,128)(2,1)}) custom-call(s32[13,30]{1,0:T(8,128)} %stack.65.meta, bf16[8,256,128]{2,1,0:T(8,128)(2,1)} %bitcast.49, bf16[128,128]{1,0:T(8,128)(2,1)} %i_hbm.1, bf16[30,256,256]{2,1,0:T(8,128)(2,1)} %r_hbm.1, bf16[4,256,128]{2,1,0:T(8,128)(2,1)} %bitcast.51, bf16[1024,128]{1,0:T(8,128)(2,1)} %ug.1, ...), custom_call_target="tpu_custom_call" | custom-call | tf_op jit(solution)/shard_map/pallas_call | solution.py:521
  110.3 1.9 %copy.14 = bf16[2048,128]{1,0:T(8,128)(2,1)} copy(bf16[2048,128]{1,0:T(8,128)(2,1)} %bitcast.50) | data formatting | bytes 1048576
  112.1 1.4 %copy.15 = bf16[128,128]{1,0:T(8,128)(2,1)} copy(bf16[128,128]{1,0:T(8,128)(2,1)} %get-tuple-element.30) | data formatting | bytes 65536
  (6 shorter events, 0.0 us)

commit v4 on v3

--- a/solution.py
+++ b/solution.py
@@ -88,6 +88,23 @@
         return came
 
 
+class Shift(Ring):
+    def send(self, distance):
+        if distance > self.steps():
+            return
+        for index, step, half in zip(self.slots[distance], (1, -1), self.halves(distance)):
+            here, there = -step * (distance - 1) % self.size, -step * distance % self.size
+            self.net.push(index, self.piece(here, half), self.piece(there, half), self.to(step))
+
+    def recv(self, distance):
+        came = []
+        for index, step, half in zip(self.slots[distance], (1, -1), self.halves(distance)):
+            back = -step * distance % self.size
+            self.net.land(index, self.piece(back, half), self.to(step))
+            came.append((back, half))
+        return came
+
+
 class Direct:
     def __init__(self, net, size, place, to, piece):
         self.net, self.size, self.place, self.to, self.piece = net, size, place, to, piece
@@ -140,9 +157,54 @@
             self.wait(index)
 
 
+def lookup(coords, count, lines):
+    slots = coords.shape[1]
+    low = lax.broadcasted_iota(jnp.int32, (slots, slots), 0)
+    high = lax.broadcasted_iota(jnp.int32, (slots, slots), 1)
+
+    def down(flat):
+        return jnp.sum(jnp.where(low == high, flat, 0), axis=1, keepdims=True)
+
+    def pick(rank, value):
+        return jnp.sum(jnp.where(rank == high, value, 0), axis=0, keepdims=True)
+
+    row, panel = coords[0:1, :], coords[1:2, :]
+    row_down, panel_down = down(row), down(panel)
+    live = (low < count).astype(jnp.int32)
+
+    def rank_of(flat, tall):
+        return jnp.sum((flat * slots + high < tall * slots + low).astype(jnp.int32), axis=1, keepdims=True)
+
+    by_row, by_panel = rank_of(row, row_down), rank_of(panel, panel_down)
+
+    def same(rank, value):
+        first = lax.broadcasted_iota(jnp.int32, (1, slots), 1) > 0
+        return ((pick(rank, value) == pick(rank + 1, value)) & first).astype(jnp.int32)
+
+    def last(value):
+        upto = jnp.sum((value <= high).astype(jnp.int32), axis=0, keepdims=True)
+        has = jnp.sum((value == high).astype(jnp.int32), axis=0, keepdims=True)
+        return jnp.maximum(upto - 1, 0), jnp.minimum(has, 1)
+
+    found = [
+        pick(by_row, low),
+        pick(by_row, row_down),
+        pick(by_row, panel_down),
+        pick(by_row, live),
+        same(by_row, row_down),
+        pick(by_panel, by_row),
+        pick(by_panel, row_down),
+        same(by_panel, panel_down),
+        *last(row_down),
+        *last(panel_down),
+    ]
+    for n, line in enumerate(found):
+        lines[n : n + 1, 0:slots] = line
+
+
 def kernel(
-    nx, nz, meta, u_hbm, i_hbm, r_hbm, ig, ug, ui, ii, unew_out, inew_out,
-    users, items, news, ratings, errors, sums, running, coupled, icoupled,
+    nx, nz, coords, count, u_hbm, i_hbm, r_hbm, ig, ug, ui, ii, unew_out, inew_out,
+    lines, meta, users, items, news_0, news_1, news_2, news_3, ratings, predicted, errors, sums, running, coupled, icoupled,
     qs, ra, sa, ta, rb, sb, tb, send_sem, recv_sem, local_sem,
 ):
     ny = NY
@@ -183,6 +245,9 @@
     peers += [other_core]
     for peer in peers:
         pl.semaphore_signal(barrier, inc=1, device_id=peer, device_id_type=MESH)
+    lookup(coords, count[0], lines)
+    to_scalars = pltpu.make_async_copy(lines, meta, local_sem.at[3 + PARTS])
+    to_scalars.start()
     pl.semaphore_wait(barrier, len(peers))
 
     net = Net(send_sem, recv_sem)
@@ -317,33 +382,34 @@
                 couple(chunk, False)
     sibling.collect()
     own[2].wait()
-
-    def whole_rank(table, row):
-        return jnp.concatenate([table[kk, xx, row] for xx in range(nx) for kk in range(2)], axis=1)
-
-    def panel_block(kk, xx, py, pz):
-        return items[kk, xx, py, pl.ds(pz, 2)].reshape(tile, width)
-
-    def error_tile(table, i):
-        row, py, pz = meta[1, i], meta[2, i], meta[3, i]
-        panel = jnp.concatenate([panel_block(kk, xx, py, pz) for xx in range(nx) for kk in range(2)], axis=1)
-        prediction = lax.dot_general(
-            whole_rank(table, row), panel, (((1,), (1,)), ((), ())), preferred_element_type=jnp.float32
+    to_scalars.wait()
+
+    def panel_block(kk, xx, i):
+        panel = meta[2, i]
+        return items[kk, xx, lax.div(panel, nz // 2), pl.ds(2 * lax.rem(panel, nz // 2), 2)].reshape(tile, width)
+
+    def product(user_blocks, chunks, i):
+        panel = jnp.concatenate([panel_block(kk, xx, i) for xx in chunks for kk in range(2)], axis=1)
+        return lax.dot_general(
+            jnp.concatenate(user_blocks, axis=1), panel, (((1,), (1,)), ((), ())), preferred_element_type=jnp.float32
         )
-        live = meta[4, i].astype(jnp.float32)
+
+    def error_of(prediction, i):
+        live = meta[3, i].astype(jnp.float32)
         return (live * (ratings[meta[0, i]].astype(jnp.float32) - prediction)).astype(jnp.bfloat16)
 
     @pl.loop(0, slots, unroll=UNROLL)
     def _(i):
-        errors[i] = error_tile(users, i)
+        row = meta[1, i]
+        blocks_of_users = [users[kk, xx, row] for xx in range(nx) for kk in range(2)]
+        errors[i] = error_of(product(blocks_of_users, range(nx), i), i)
 
     running[...] = jnp.zeros_like(running)
 
     @pl.loop(0, slots, unroll=UNROLL)
     def _(i):
-        block = panel_block(k, x, meta[2, i], meta[3, i])
-        added = jnp.dot(errors[i], block, preferred_element_type=jnp.float32)
-        total = running[...] * meta[5, i].astype(jnp.float32) + added
+        added = jnp.dot(errors[i], panel_block(k, x, i), preferred_element_type=jnp.float32)
+        total = running[...] * meta[4, i].astype(jnp.float32) + added
         running[...] = total
         sums[i] = total
 
@@ -353,62 +419,77 @@
 
     per = row_tiles // PARTS
     rings = []
+    own_news = []
+    news = [news_0, news_1, news_2, news_3]
     out_copies = []
     for part in range(PARTS):
 
         @pl.loop(part * per, (part + 1) * per)
         def _(r):
-            observed = sums[meta[9, r]] * meta[10, r].astype(jnp.float32)
+            observed = sums[meta[8, r]] * meta[9, r].astype(jnp.float32)
             factors = users[k, x, r].astype(jnp.float32)
             gradient = observed - UNOBSERVED * coupled[r] - REGULAR * factors
-            news[k, x, r] = newton(factors, gradient, ui[...])
-
-        def piece(chunk, half, kk=None, part=part):
+            news[0][k, r] = newton(factors, gradient, ui[...])
+
+        def piece(back, half, kk=None, part=part):
             kk = k if kk is None else kk
             if half is None:
-                return news.at[kk, chunk, pl.ds(part * per, per)]
-            return news.at[kk, chunk, pl.ds(part * per, per), pl.ds(half * (tile // 2), tile // 2)]
-
-        ring = Ring(net, nx, x, along_x, piece)
+                return news[back].at[kk, pl.ds(part * per, per)]
+            return news[back].at[kk, pl.ds(part * per, per), pl.ds(half * (tile // 2), tile // 2)]
+
+        ring = Shift(net, nx, x, along_x, piece)
         ring.send(1)
-        sibling.hand(functools.partial(piece, x, None))
+        own_news.append(sibling.hand(functools.partial(piece, 0, None)))
         rings.append(ring)
         copy = pltpu.make_async_copy(
-            news.at[k, x, pl.ds(part * per, per)], unew_out.at[pl.ds(part * per, per)], local_sem.at[3 + part]
+            news[0].at[k, pl.ds(part * per, per)], unew_out.at[pl.ds(part * per, per)], local_sem.at[3 + part]
         )
         copy.start()
         out_copies.append(copy)
     mine = jnp.concatenate([items[kk, xx, y, z] for xx in range(nx) for kk in range(2)], axis=1)
     icoupled[...] = jnp.dot(mine, ug[...], preferred_element_type=jnp.float32)
 
-    for step in range(1, nx // 2 + 1):
-        for ring in rings:
-            came = ring.recv(step)
-            ring.send(step + 1)
-            pass_on(ring, came)
-    sibling.collect()
-
-    @pl.loop(0, slots, unroll=UNROLL)
-    def _(i):
-        errors[i] = error_tile(news, i)
+    def predict_from(backs, begin, end):
+        @pl.loop(0, slots, unroll=UNROLL)
+        def _(i):
+            row = meta[1, i]
+            blocks_of_users = [news[back][kk, row] for back in backs for kk in range(2)]
+            value = product(blocks_of_users, [lax.rem(x + back, nx) for back in backs], i)
+            value = value if begin else predicted[i] + value
+            if end:
+                errors[i] = error_of(value, i)
+            else:
+                predicted[i] = value
+
+    hands = own_news
+    for step in range(nx // 2 + 1):
+        if step > 0:
+            hands = []
+            for ring in rings:
+                came = ring.recv(step)
+                ring.send(step + 1)
+                hands += pass_on(ring, came)
+        for hand in hands:
+            sibling.wait(hand)
+        predict_from(sorted({step, (nx - step) % nx}), step == 0, step == nx // 2)
 
     running[...] = jnp.zeros_like(running)
 
     @pl.loop(0, slots, unroll=UNROLL)
     def _(i):
         added = lax.dot_general(
-            errors[meta[6, i]],
-            news[k, x, meta[7, i]],
+            errors[meta[5, i]],
+            news[0][k, meta[6, i]],
             (((0,), (0,)), ((), ())),
             preferred_element_type=jnp.float32,
         )
-        total = running[...] * meta[8, i].astype(jnp.float32) + added
+        total = running[...] * meta[7, i].astype(jnp.float32) + added
         running[...] = total
         sums[i] = total
 
     @pl.loop(0, panels)
     def _(p):
-        panel = sums[meta[11, p]] * meta[12, p].astype(jnp.float32)
+        panel = sums[meta[10, p]] * meta[11, p].astype(jnp.float32)
         pair = panel.astype(jnp.bfloat16).reshape(2, owner_rows, width)
         qs[lax.div(p, nz // 2), pl.ds(2 * lax.rem(p, nz // 2), 2)] = pair
 
@@ -461,58 +542,11 @@
     net.drain()
 
 
-def lookup(tile_coords, tile_count, row_tiles, panel_count, nz):
-    count = tile_coords.shape[0]
-    row, panel = tile_coords[:, 0], tile_coords[:, 1]
-    slot = lax.iota(jnp.int32, count)
-    live = (slot < tile_count[0]).astype(jnp.int32)
-
-    def rank_of(value):
-        key = value * count + slot
-        return jnp.sum((key[None, :] < key[:, None]).astype(jnp.int32), axis=1)
-
-    def sort_by(rank, value):
-        return jnp.sum(jnp.where(rank[None, :] == slot[:, None], value[None, :], 0), axis=1)
-
-    def same(value):
-        return jnp.concatenate([jnp.zeros((1,), jnp.int32), (value[1:] == value[:-1]).astype(jnp.int32)])
-
-    def last(value, size):
-        ids = lax.iota(jnp.int32, size)[:, None]
-        upto = jnp.sum((value[None, :] <= ids).astype(jnp.int32), axis=1)
-        has = jnp.any(value[None, :] == ids, axis=1).astype(jnp.int32)
-        return jnp.maximum(upto - 1, 0), has
-
-    by_row, by_panel = rank_of(row), rank_of(panel)
-    sorted_row, sorted_panel = sort_by(by_row, row), sort_by(by_row, panel)
-    last_row, has_row = last(row, row_tiles)
-    last_panel, has_panel = last(panel, panel_count)
-    lines = [
-        sort_by(by_row, slot),
-        sorted_row,
-        sorted_panel // (nz // 2),
-        2 * (sorted_panel % (nz // 2)),
-        sort_by(by_row, live),
-        same(sorted_row),
-        sort_by(by_panel, by_row),
-        sort_by(by_panel, row),
-        same(sort_by(by_panel, panel)),
-        last_row,
-        has_row,
-        last_panel,
-        has_panel,
-    ]
-    wide = max(count, row_tiles, panel_count)
-    return jnp.stack([jnp.pad(line, (0, wide - line.shape[0])) for line in lines])
-
-
 def local(nx, nz, user_factors, item_factors, ratings, tile_coords, tile_count, item_gram, user_gram, user_inverse, item_inverse):
     user_rows, width = user_factors.shape
     owner_rows = item_factors.shape[0]
     slots, tile, _ = ratings.shape
     row_tiles = user_rows // tile
-    panel_count = NY * nz * owner_rows // tile
-    meta = lookup(tile_coords, tile_count, row_tiles, panel_count, nz)
     na = owner_rows * 3 // 8 // 16 * 16
     nb = owner_rows - na
     bf16, f32 = jnp.bfloat16, jnp.float32
@@ -524,13 +558,16 @@
             jax.ShapeDtypeStruct((row_tiles, tile, width), bf16),
             jax.ShapeDtypeStruct((owner_rows, width), bf16),
         ),
-        in_specs=[pl.BlockSpec(memory_space=pltpu.SMEM), hbm, hbm, hbm, vmem, vmem, vmem, vmem],
+        in_specs=[vmem, pl.BlockSpec(memory_space=pltpu.SMEM), hbm, hbm, hbm, vmem, vmem, vmem, vmem],
         out_specs=(hbm, vmem),
         scratch_shapes=[
+            pltpu.VMEM((16, 128), jnp.int32),
+            pltpu.SMEM((16, 128), jnp.int32),
             pltpu.VMEM((2, nx, row_tiles, tile, width), bf16),
             pltpu.VMEM((2, nx, NY, nz, owner_rows, width), bf16),
-            pltpu.VMEM((2, nx, row_tiles, tile, width), bf16),
+            *[pltpu.VMEM((2, row_tiles, tile, width), bf16)] * 4,
             pltpu.VMEM((slots, tile, tile), bf16),
+            pltpu.VMEM((slots, tile, tile), f32),
             pltpu.VMEM((slots, tile, tile), bf16),
             pltpu.VMEM((slots, tile, width), f32),
             pltpu.VMEM((tile, width), f32),
@@ -545,13 +582,14 @@
             pltpu.VMEM((nz - 1, nb, width), bf16),
             pltpu.SemaphoreType.DMA((SEMS,)),
             pltpu.SemaphoreType.DMA((SEMS,)),
-            pltpu.SemaphoreType.DMA((3 + PARTS,)),
+            pltpu.SemaphoreType.DMA((4 + PARTS,)),
         ],
         compiler_params=pltpu.CompilerParams(
             collective_id=0, has_side_effects=True, vmem_limit_bytes=56 * 1024 * 1024
         ),
     )(
-        meta,
+        tile_coords.T,
+        tile_count,
         user_factors.reshape(row_tiles, tile, width),
         item_factors,
         ratings,

time: 114 us -> 109 us (0.956)
  other arithmetic: 2.73 us -> 0 us
  Pallas kernels: 105 us -> 103 us
  local copies, waits for them, and re-layouts: 4.47 us -> 3.24 us
    pallas_call x1, Pallas kernels: 105 us -> 103 us  [local(): pl.pallas_call(functools.partial(kernel, nx, nz), out_shape=(jax.ShapeDty...]
    another operation x2 -> x0, local copies, waits for them, and re-layouts: 1.23 us -> none  [lookup(): jnp.stack([jnp.pad(line, (0, wide - line.shape[0])) for line in lines])]
where the time goes in v4:
time: 109 us; the launch traced here: 108 us
  Pallas kernels  103 us (94%)
  local copies, waits for them, and re-layouts  3.24 us (3%)
  between operations  1.29 us (1%)
    pallas_call x1, Pallas kernels, local(): pl.pallas_call(functools.partial(kernel, nx, nz), out_shape=(jax.ShapeDty...  103 us
    unnamed x2, local copies, waits for them, and re-layouts  3.24 us

profile of v4, /device:TPU:2, one launch (start us, length us, event | category | flops | bytes accessed | tf_op | source)
XLA Modules:
  0.0 107.8 jit_solution(6446058919365668723)
XLA Ops:
  1.3 103.3 %shard_map.104 = (bf16[8,256,128]{2,1,0:T(8,128)(2,1)}, bf16[128,128]{1,0:T(8,128)(2,1)}) custom-call(s32[2,30]{1,0:T(2,128)} %bitcast.7, s32[1]{0:T(128)S(6)} %copy.13.count, bf16[8,256,128]{2,1,0:T(8,128)(2,1)} %bitcast.4, bf16[128,128]{1,0:T(8,128)(2,1)} %i_hbm.1, bf16[30,256,256]{2,1,0:T(8,128)(2,1)} %r_hbm.1, bf16[4,256,128]{2,1,0:T(8,128)(2,1)} %bitcast.6, ...), custom_call_target="tpu_custom_call" | custom-call | tf_op jit(solution)/shard_map/pallas_call | solution.py:555
  104.6 1.9 %copy.14 = bf16[2048,128]{1,0:T(8,128)(2,1)} copy(bf16[2048,128]{1,0:T(8,128)(2,1)} %bitcast.5) | data formatting | bytes 1048576
  106.4 1.4 %copy.15 = bf16[128,128]{1,0:T(8,128)(2,1)} copy(bf16[128,128]{1,0:T(8,128)(2,1)} %get-tuple-element.9) | data formatting | bytes 65536

commit v5 on v4

--- a/solution.py
+++ b/solution.py
@@ -15,6 +15,7 @@
 PARTS = 4
 SEMS = 240
 UNROLL = 5
+LANES = 2
 
 
 class Net:
@@ -314,9 +315,17 @@
                 arrived(step, came)
                 entry[2] += 1
 
-    def second_z(step, came):
-        if step == az.steps():
-            sibling.hand(functools.partial(item_piece, 0, whole, whole, None))
+    def second_z(lane):
+        def piece(n, half, kk=None):
+            kk, size = k if kk is None else kk, nx // LANES
+            if half is None:
+                return items.at[kk, pl.ds(lane * size, size), :, n, rows_of(0, None)]
+            if size > 1:
+                return items.at[kk, pl.ds(lane * size + half * (size // 2), size // 2), :, n, rows_of(0, None)]
+            return items.at[kk, pl.ds(lane * size, size), :, n, pl.ds(half * (split // 2), split // 2)]
+
+        ring = Ring(net, nz, z, along_z, piece)
+        start(1, ring, lambda step, came: pass_on(ring, came))
 
     def second_y(zz, is_last):
         def arrived(step, came):
@@ -327,7 +336,9 @@
 
     def first_y(step, came):
         if step == ay.steps():
-            start(1, az, second_z)
+            for lane in range(LANES):
+                second_z(lane)
+            sibling.hand(functools.partial(item_piece, 0, whole, z, None))
 
     def first_z(step, came):
         for n, chunk in enumerate(came):
@@ -344,13 +355,12 @@
 
     ay = Direct(net, ny, y, along_y, lambda n, h: item_piece(0, n, z, h))
     bz = Direct(net, nz, z, along_z, lambda n, h: item_piece(1, y, n, h))
-    az = Ring(net, nz, z, along_z, lambda n, h: item_piece(0, whole, n, h))
     start(0, ay, first_y)
     start(0, bz, first_z)
     second_y(z, bz.steps() == 0)
     if ay.steps() == 0:
-        start(1, az, second_z)
-    waves = max(ay.steps() + az.steps(), bz.steps() + ny // 2)
+        first_y(0, [])
+    waves = max(ay.steps() + nz // 2, bz.steps() + ny // 2)
     user_hands = []
     met = xu_step = 0
     for number in range(1, waves + 1):

time: 109 us -> 108 us (level)
  no operation moved by 1% of the time
where the time goes in v5:
time: 108 us; the launch traced here: 107 us
  Pallas kernels  103 us (95%)
  local copies, waits for them, and re-layouts  3.24 us (3%)
  between operations  1.29 us (1%)
    pallas_call x1, Pallas kernels, local(): pl.pallas_call(functools.partial(kernel, nx, nz), out_shape=(jax.ShapeDty...  103 us
    unnamed x2, local copies, waits for them, and re-layouts  3.24 us

profile of v5, /device:TPU:2, one launch (start us, length us, event | category | flops | bytes accessed | tf_op | source)
XLA Modules:
  0.0 107.5 jit_solution(994393313292400346)
XLA Ops:
  1.3 102.9 %shard_map.104 = (bf16[8,256,128]{2,1,0:T(8,128)(2,1)}, bf16[128,128]{1,0:T(8,128)(2,1)}) custom-call(s32[2,30]{1,0:T(2,128)} %bitcast.7, s32[1]{0:T(128)S(6)} %copy.13.count, bf16[8,256,128]{2,1,0:T(8,128)(2,1)} %bitcast.4, bf16[128,128]{1,0:T(8,128)(2,1)} %i_hbm.1, bf16[30,256,256]{2,1,0:T(8,128)(2,1)} %r_hbm.1, bf16[4,256,128]{2,1,0:T(8,128)(2,1)} %bitcast.6, ...), custom_call_target="tpu_custom_call" | custom-call | tf_op jit(solution)/shard_map/pallas_call | solution.py:565
  104.2 1.9 %copy.14 = bf16[2048,128]{1,0:T(8,128)(2,1)} copy(bf16[2048,128]{1,0:T(8,128)(2,1)} %bitcast.5) | data formatting | bytes 1048576
  106.1 1.4 %copy.15 = bf16[128,128]{1,0:T(8,128)(2,1)} copy(bf16[128,128]{1,0:T(8,128)(2,1)} %get-tuple-element.9) | data formatting | bytes 65536

commit v6 on v5

--- a/solution.py
+++ b/solution.py
@@ -87,6 +87,57 @@
             self.net.land(index, self.piece(chunk, half), self.to(step))
             came.append((chunk, half))
         return came
+
+
+def cut(size, half):
+    return pl.ds(0, size) if half is None else pl.ds(half * (size // 2), size // 2)
+
+
+class Scatter:
+    def __init__(self, net, size, place, to, where, inner, table, landing, relayed, halves):
+        self.net, self.size, self.place, self.to, self.where, self.inner = net, size, place, to, where, inner
+        self.table, self.landing, self.relayed = table, landing, relayed
+        self.far = size // 2 - 1 if size >= 4 and halves else 0
+        self.steps = [s for s in range(1, size) if not (self.far and 2 * s == size)]
+        self.slots = {s: [net.slot(), net.slot()] for s in self.steps}
+        self.passing = [net.slot(), net.slot()]
+        self.turn = {0: self.far, 1: size - self.far}
+
+    def chunk(self, step):
+        return lax.rem(self.place + step, self.size)
+
+    def push(self, step, half):
+        source = self.table.at[self.where(self.chunk(step), half)]
+        target = self.landing.at[step - 1] if half is None else self.landing.at[(step - 1, *self.inner(half))]
+        self.net.push(self.slots[step][half or 0], source, target, self.to(step))
+
+    def send(self):
+        if self.far:
+            for half, way in ((0, 1), (1, -1)):
+                source = self.table.at[self.where(self.chunk(self.size // 2), half)]
+                self.net.push(self.passing[half], source, self.relayed.at[half], self.to(way))
+        for step in self.steps:
+            if not self.far or step not in self.turn.values():
+                self.push(step, None)
+        for half in (0, 1) if self.far else ():
+            self.push(self.turn[half], 1 - half)
+
+    def relay(self):
+        for half, way in ((0, 1), (1, -1)) if self.far else ():
+            self.net.land(self.passing[half], self.relayed.at[half], self.to(way))
+            place = self.where(self.chunk(self.turn[half]), half)
+            value = self.table[place].astype(jnp.float32) + self.relayed[half].astype(jnp.float32)
+            self.table[place] = value.astype(jnp.bfloat16)
+            self.push(self.turn[half], half)
+
+    def land(self):
+        for step in self.steps:
+            if not self.far or step not in self.turn.values():
+                self.net.land(self.slots[step][0], self.landing.at[step - 1], self.to(step))
+            else:
+                for half in (0, 1):
+                    view = self.landing.at[(step - 1, *self.inner(half))]
+                    self.net.land(self.slots[step][half], view, self.to(step))
 
 
 class Shift(Ring):
@@ -206,7 +257,7 @@
 def kernel(
     nx, nz, coords, count, u_hbm, i_hbm, r_hbm, ig, ug, ui, ii, unew_out, inew_out,
     lines, meta, users, items, news_0, news_1, news_2, news_3, ratings, predicted, errors, sums, running, coupled, icoupled,
-    qs, ra, sa, ta, rb, sb, tb, send_sem, recv_sem, local_sem,
+    qs, ra, sa, ta, rb, sb, tb, yb, za, send_sem, recv_sem, local_sem,
 ):
     ny = NY
     u = lax.axis_index("users")
@@ -505,28 +556,24 @@
 
     na = ra.shape[2]
     a_rows, b_rows = pl.ds(0, na), pl.ds(na, owner_rows - na)
-    b_slots = [net.slot() for _ in range(1, ny)]
-    a_slots = [net.slot() for _ in range(1, nz)]
-    for step in range(1, ny):
-        to = lax.rem(y + step, ny)
-        net.push(b_slots[step - 1], qs.at[to, :, b_rows], rb.at[step - 1], along_y(step))
-    for step in range(1, nz):
-        to = lax.rem(z + step, nz)
-        net.push(a_slots[step - 1], qs.at[:, to, a_rows], ra.at[step - 1], along_z(step))
-    for step in range(1, nz):
-        net.land(a_slots[step - 1], ra.at[step - 1], along_z(step))
+    b_part = Scatter(net, ny, y, along_y, lambda n, h: (n, cut(nz, h), b_rows), lambda h: (cut(nz, h),), qs, rb, yb, nz > 1)
+    a_part = Scatter(net, nz, z, along_z, lambda n, h: (cut(ny, h), n, a_rows), lambda h: (cut(ny, h),), qs, ra, za, ny > 1)
+    b_part.send()
+    a_part.send()
+    b_part.relay()
+    a_part.relay()
+    a_part.land()
     total = qs[:, z, a_rows].astype(jnp.float32)
-    for step in range(1, nz):
+    for step in a_part.steps:
         total = total + ra[step - 1].astype(jnp.float32)
     sa[...] = total.astype(jnp.bfloat16)
     c_slots = [net.slot() for _ in range(1, ny)]
     for step in range(1, ny):
         to = lax.rem(y + step, ny)
         net.push(c_slots[step - 1], sa.at[to], ta.at[step - 1], along_y(step))
-    for step in range(1, ny):
-        net.land(b_slots[step - 1], rb.at[step - 1], along_y(step))
+    b_part.land()
     total = qs[y, :, b_rows].astype(jnp.float32)
-    for step in range(1, ny):
+    for step in b_part.steps:
         total = total + rb[step - 1].astype(jnp.float32)
     sb[...] = total.astype(jnp.bfloat16)
     d_slots = [net.slot() for _ in range(1, nz)]
@@ -557,7 +604,7 @@
     owner_rows = item_factors.shape[0]
     slots, tile, _ = ratings.shape
     row_tiles = user_rows // tile
-    na = owner_rows * 3 // 8 // 16 * 16
+    na = owner_rows // 4
     nb = owner_rows - na
     bf16, f32 = jnp.bfloat16, jnp.float32
     vmem = pl.BlockSpec(memory_space=pltpu.VMEM)
@@ -590,6 +637,8 @@
             pltpu.VMEM((max(NY - 1, 1), nz, nb, width), bf16),
             pltpu.VMEM((nz, nb, width), bf16),
             pltpu.VMEM((nz - 1, nb, width), bf16),
+            pltpu.VMEM((2, max(nz // 2, 1), nb, width), bf16),
+            pltpu.VMEM((2, max(NY // 2, 1), na, width), bf16),
             pltpu.SemaphoreType.DMA((SEMS,)),
             pltpu.SemaphoreType.DMA((SEMS,)),
             pltpu.SemaphoreType.DMA((4 + PARTS,)),

time: 108 us -> 106 us (0.981)
  Pallas kernels: 103 us -> 101 us
    pallas_call x1, Pallas kernels: 103 us -> 101 us  [local(): pl.pallas_call(functools.partial(kernel, nx, nz), out_shape=(jax.ShapeDty...]
where the time goes in v6:
time: 106 us
  Pallas kernels  101 us (95%)
  local copies, waits for them, and re-layouts  3.24 us (3%)
  between operations  1.29 us (1%)
    pallas_call x1, Pallas kernels, local(): pl.pallas_call(functools.partial(kernel, nx, nz), out_shape=(jax.ShapeDty...  101 us
    unnamed x2, local copies, waits for them, and re-layouts  3.24 us

profile of v6, /device:TPU:2, one launch (start us, length us, event | category | flops | bytes accessed | tf_op | source)
XLA Modules:
  0.0 105.7 jit_solution(6801174555668597589)
XLA Ops:
  1.3 101.2 %shard_map.104 = (bf16[8,256,128]{2,1,0:T(8,128)(2,1)}, bf16[128,128]{1,0:T(8,128)(2,1)}) custom-call(s32[2,30]{1,0:T(2,128)} %bitcast.7, s32[1]{0:T(128)S(6)} %copy.13.count, bf16[8,256,128]{2,1,0:T(8,128)(2,1)} %bitcast.4, bf16[128,128]{1,0:T(8,128)(2,1)} %i_hbm.1, bf16[30,256,256]{2,1,0:T(8,128)(2,1)} %r_hbm.1, bf16[4,256,128]{2,1,0:T(8,128)(2,1)} %bitcast.6, ...), custom_call_target="tpu_custom_call" | custom-call | tf_op jit(solution)/shard_map/pallas_call | solution.py:612
  102.5 1.9 %copy.14 = bf16[2048,128]{1,0:T(8,128)(2,1)} copy(bf16[2048,128]{1,0:T(8,128)(2,1)} %bitcast.5) | data formatting | bytes 1048576
  104.3 1.4 %copy.15 = bf16[128,128]{1,0:T(8,128)(2,1)} copy(bf16[128,128]{1,0:T(8,128)(2,1)} %get-tuple-element.9) | data formatting | bytes 65536

commit v7 on v6

--- a/solution.py
+++ b/solution.py
@@ -14,7 +14,7 @@
 NY = 4
 PARTS = 4
 SEMS = 240
-UNROLL = 5
+UNROLL = 10
 LANES = 2
 
 

time: 106 us -> 104 us (0.981)
  Pallas kernels: 101 us -> 99.3 us
    pallas_call x1, Pallas kernels: 101 us -> 99.3 us  [local(): pl.pallas_call(functools.partial(kernel, nx, nz), out_shape=(jax.ShapeDty...]
where the time goes in v7:
time: 104 us
  Pallas kernels  99.3 us (95%)
  local copies, waits for them, and re-layouts  3.24 us (3%)
  between operations  1.29 us (1%)
    pallas_call x1, Pallas kernels, local(): pl.pallas_call(functools.partial(kernel, nx, nz), out_shape=(jax.ShapeDty...  99.3 us
    unnamed x2, local copies, waits for them, and re-layouts  3.24 us

profile of v7, /device:TPU:2, one launch (start us, length us, event | category | flops | bytes accessed | tf_op | source)
XLA Modules:
  0.0 103.8 jit_solution(5641066480825278519)
XLA Ops:
  1.3 99.3 %shard_map.104 = (bf16[8,256,128]{2,1,0:T(8,128)(2,1)}, bf16[128,128]{1,0:T(8,128)(2,1)}) custom-call(s32[2,30]{1,0:T(2,128)} %bitcast.7, s32[1]{0:T(128)S(6)} %copy.13.count, bf16[8,256,128]{2,1,0:T(8,128)(2,1)} %bitcast.4, bf16[128,128]{1,0:T(8,128)(2,1)} %i_hbm.1, bf16[30,256,256]{2,1,0:T(8,128)(2,1)} %r_hbm.1, bf16[4,256,128]{2,1,0:T(8,128)(2,1)} %bitcast.6, ...), custom_call_target="tpu_custom_call" | custom-call | tf_op jit(solution)/shard_map/pallas_call | solution.py:612
  100.6 1.9 %copy.14 = bf16[2048,128]{1,0:T(8,128)(2,1)} copy(bf16[2048,128]{1,0:T(8,128)(2,1)} %bitcast.5) | data formatting | bytes 1048576
  102.4 1.4 %copy.15 = bf16[128,128]{1,0:T(8,128)(2,1)} copy(bf16[128,128]{1,0:T(8,128)(2,1)} %get-tuple-element.9) | data formatting | bytes 65536

commit v8 on v7

--- a/solution.py
+++ b/solution.py
@@ -14,7 +14,7 @@
 NY = 4
 PARTS = 4
 SEMS = 240
-UNROLL = 10
+UNROLL = 15
 LANES = 2
 
 

time: 104 us -> 103 us (level)
  Pallas kernels: 99.3 us -> 98.1 us
    pallas_call x1, Pallas kernels: 99.3 us -> 98.1 us  [local(): pl.pallas_call(functools.partial(kernel, nx, nz), out_shape=(jax.ShapeDty...]
where the time goes in v8:
time: 103 us
  Pallas kernels  98.1 us (95%)
  local copies, waits for them, and re-layouts  3.24 us (3%)
  between operations  1.29 us (1%)
    pallas_call x1, Pallas kernels, local(): pl.pallas_call(functools.partial(kernel, nx, nz), out_shape=(jax.ShapeDty...  98.1 us
    unnamed x2, local copies, waits for them, and re-layouts  3.24 us

profile of v8, /device:TPU:2, one launch (start us, length us, event | category | flops | bytes accessed | tf_op | source)
XLA Modules:
  0.0 102.6 jit_solution(10955132604755871806)
XLA Ops:
  1.3 98.1 %shard_map.104 = (bf16[8,256,128]{2,1,0:T(8,128)(2,1)}, bf16[128,128]{1,0:T(8,128)(2,1)}) custom-call(s32[2,30]{1,0:T(2,128)} %bitcast.7, s32[1]{0:T(128)S(6)} %copy.13.count, bf16[8,256,128]{2,1,0:T(8,128)(2,1)} %bitcast.4, bf16[128,128]{1,0:T(8,128)(2,1)} %i_hbm.1, bf16[30,256,256]{2,1,0:T(8,128)(2,1)} %r_hbm.1, bf16[4,256,128]{2,1,0:T(8,128)(2,1)} %bitcast.6, ...), custom_call_target="tpu_custom_call" | custom-call | tf_op jit(solution)/shard_map/pallas_call | solution.py:612
  99.4 1.9 %copy.14 = bf16[2048,128]{1,0:T(8,128)(2,1)} copy(bf16[2048,128]{1,0:T(8,128)(2,1)} %bitcast.5) | data formatting | bytes 1048576
  101.2 1.4 %copy.15 = bf16[128,128]{1,0:T(8,128)(2,1)} copy(bf16[128,128]{1,0:T(8,128)(2,1)} %get-tuple-element.9) | data formatting | bytes 65536
